TPU v7x, 32 devices: a whole 2x2x4 slice. The times are simulated.
32 devices in a mesh: aux: 8 (over z, x), grp: 4 (over y, core).
Axes of the slice: x: 2, y: 2, z: 4, core: 2. Of those that a mesh axis runs over, the one named last changes fastest.
Arguments:
- occ_blocks: bfloat16 [32, 128, 256], P('aux'), may hold values from -6 to 6
- virt_blocks: bfloat16 [32, 128, 256], P('aux'), may hold values from -6 to 6
- three_center: bfloat16 [16384, 1024], P(('aux', 'grp')), may hold values from -0.1875 to 0.1875
- blk_index: int32 [8, 8], P(None, 'aux'), may hold values from 0 to 3
- blk_live: int32 [8, 8], P(None, 'aux'), may hold values 0 or 1
- live_counts: int32 [16], replicated, may hold values from 1 to 16
Outputs:
- polarizability: float32 [16384, 2048], P(('aux', 'grp'))
All inputs are finite; a program needn't handle non-finite values. No bound on the sum of `blk_live` on one device may be relied on, other than what follows from the above.
Results may differ from a plain program's by a relative error of at most 0.0041.
Values may be sent and summed in bfloat16 or wider, within the bound.
A program may use at most 128 MiB of HBM per device.

v0:
```python
import math

import jax
import jax.numpy as jnp
from jax import lax
from jax.sharding import PartitionSpec as P

group_width = 16


def body(occ_blocks, virt_blocks, three_center, blk_index, blk_live, live_counts):
    aux_count = lax.axis_size("aux")
    local_count = occ_blocks.shape[0]
    block_size = occ_blocks.shape[1]
    width = occ_blocks.shape[2]
    scale = 1.0 / math.sqrt(width)
    picked = blk_index[:, 0][:, None] == jnp.arange(local_count, dtype=jnp.int32)[None, :]
    chosen = (picked & (blk_live[:, 0][:, None] == 1)).astype(jnp.bfloat16)
    columns = jnp.arange(width, dtype=jnp.int32)
    group_ids = jnp.arange(live_counts.shape[0], dtype=jnp.int32)
    owner_hit = (columns // group_width)[:, None] == group_ids[None, :]
    limits = jnp.sum(jnp.where(owner_hit, live_counts[None, :], 0), axis=1)
    col_mask = (columns % group_width < limits).astype(jnp.float32)
    flat_occ = occ_blocks.reshape(local_count, block_size * width)
    flat_virt = virt_blocks.reshape(local_count, block_size * width)
    send_occ = jnp.dot(chosen, flat_occ, preferred_element_type=jnp.float32).astype(jnp.bfloat16)
    send_virt = jnp.dot(chosen, flat_virt, preferred_element_type=jnp.float32).astype(jnp.bfloat16)
    got_occ, got_virt = (
        lax.all_to_all(send_occ, "aux", split_axis=0, concat_axis=0, tiled=True),
        lax.all_to_all(send_virt, "aux", split_axis=0, concat_axis=0, tiled=True),
    )
    prod_occ = jnp.dot(
        three_center,
        got_occ.reshape(aux_count * block_size, width),
        preferred_element_type=jnp.float32,
    )
    prod_virt = jnp.dot(
        three_center,
        got_virt.reshape(aux_count * block_size, width),
        preferred_element_type=jnp.float32,
    )
    half_occ = (prod_occ * col_mask).astype(jnp.bfloat16)
    half_virt = prod_virt.astype(jnp.bfloat16)
    return (
        lax.dot_general(
            half_occ,
            lax.all_gather(half_virt, "grp", axis=0, tiled=True),
            (((1,), (1,)), ((), ())),
            preferred_element_type=jnp.float32,
        )
        * scale
    )


def solution(mesh):
    placed = (
        P("aux", None, None),
        P("aux", None, None),
        P(("aux", "grp"), None),
        P(None, "aux"),
        P(None, "aux"),
        P(),
    )
    return jax.shard_map(
        body, mesh=mesh, in_specs=placed, out_specs=P(("aux", "grp"), None), check_vma=False
    )
```

profile of v0, /device:TPU:0, one launch (start us, length us, event | category | flops | bytes accessed | tf_op | source)
XLA Modules:
  0.0 74.0 jit_solution(10946220920309949540)
XLA Ops:
  6.5 0.0 copy-start
  6.5 0.0 all-gather.2.cloned.1.call-start
  6.5 0.7 %compare_bitcast_fusion = pred[8]{0:T(512)(128)(4,1)S(1)} fusion(s32[8,1]{0,1:T(1,128)} %param.10), kind=kLoop, calls=%fused_computation.21 | loop fusion | flops 8 | bytes 40 | tf_op jit(solution)/shard_map/and | solution.py:18
  7.3 1.2 %copy.14 = bf16[1,4,128,256]{3,1,2,0:T(4,128)(2,1)S(1)} copy(bf16[1,4,128,256]{3,2,1,0:T(8,128)(2,1)} %bitcast.22) | data formatting | bytes 524288
  8.4 1.0 %fusion.1 = bf16[8,1,32768]{2,0,1:T(8,128)(2,1)S(1)} fusion(bf16[4,32768]{1,0:T(4,128)(2,1)S(1)} %bitcast.21, s32[8]{0:T(128)} %bitcast.24, pred[8]{0:T(512)(128)(4,1)S(1)} %compare_bitcast_fusion), kind=kOutput, calls=%fused_computation.3 | convolution fusion | flops 2359360 | bytes 786472 | tf_op jit(solution)/shard_map/dot_general | solution.py:27
  9.5 0.5 broadcast.63
  10.0 1.0 %reduce.2 = bf16[8,32768]{1,0:T(8,128)(2,1)S(1)} reduce(bf16[8,1,32768]{2,0,1:T(8,128)(2,1)S(1)} %fusion.1, bf16[]{:T(256)} %broadcast.63), dimensions={1}, to_apply=%copy.12.reduce_sub_computation | reduce | bytes 1048578 | tf_op jit(solution)/shard_map/all_to_all | solution.py:30
  11.0 0.0 copy-start.1
  11.0 0.4 reshape.51
  11.4 0.0 copy-start.2
  11.4 21.6 %all_to_all.18 = bf16[8,2,16384]{2,1,0:T(2,128)(2,1)S(1)} all-to-all(bf16[8,2,16384]{2,1,0:T(2,128)(2,1)S(1)} %reshape.51), channel_id=1, replica_groups=mesh['aux'=8,'grp'=4] {'aux'}, dimensions={0} | all-to-all | bytes 1048576 | tf_op jit(solution)/shard_map/all_to_all | solution.py:30
  33.0 0.5 reshape.52
  33.5 3.2 %reduce.1 = bf16[8,32768]{1,0:T(8,128)(2,1)S(1)} reduce(bf16[8,1,32768]{2,1,0:T(2,128)(2,1)S(1)} %reshape.52, bf16[]{:T(256)} %constant.39), dimensions={1}, to_apply=%all_to_all.15.reduce_sub_computation | reduce | bytes 1048578 | tf_op jit(solution)/shard_map/all_to_all | solution.py:30
  36.7 0.0 copy-start.3
  36.7 0.2 reshape.48
  37.0 0.0 copy-done
  37.0 1.2 %fusion.3 = bf16[512,256]{0,1:T(8,128)(2,1)} fusion(bf16[1024,256]{1,0:T(8,128)(2,1)S(1)} %reshape.48, bf16[512,1024]{1,0:T(8,128)(2,1)S(1)} %copy-done), kind=kOutput, calls=%fused_computation.8 | convolution fusion | flops 268566528 | bytes 1835008 | tf_op jit(solution)/shard_map/dot_general | solution.py:37
  38.2 0.0 all-gather.2.cloned.1.call-update
  38.2 0.0 copy-done.1
  38.2 0.2 copy.13
  38.4 0.0 copy-done.2
  38.4 0.4 fusion
  38.8 1.0 %reduce.3 = bf16[8,32768]{1,0:T(8,128)(2,1)S(1)} reduce(bf16[8,1,32768]{2,0,1:T(8,128)(2,1)S(1)} %fusion, bf16[]{:T(256)} %broadcast.63), dimensions={1}, to_apply=%copy.11.reduce_sub_computation | reduce | bytes 1048578 | tf_op jit(solution)/shard_map/all_to_all | solution.py:29
  39.8 1.2 %reshape.53 = bf16[8,2,16384]{2,1,0:T(2,128)(2,1)} reshape(bf16[8,32768]{1,0:T(8,128)(2,1)S(1)} %reduce.3) | data formatting | bytes 1048576
  41.0 3.6 %all-to-all-start = ((bf16[8,2,16384]{2,1,0:T(2,128)(2,1)}), bf16[8,2,16384]{2,1,0:T(2,128)(2,1)S(1)}, u32[]{:S(2)}, u32[]{:S(2)}) async-start(bf16[8,2,16384]{2,1,0:T(2,128)(2,1)} %reshape.53), calls=%async_computation | async-start | bytes 1048576 | tf_op jit(solution)/shard_map/all_to_all | solution.py:29
  44.6 0.0 copy-done.3
  44.6 0.1 select_reduce_fusion
  44.7 14.1 %all-to-all-done = bf16[8,2,16384]{2,1,0:T(2,128)(2,1)S(1)} async-done(((bf16[8,2,16384]{2,1,0:T(2,128)(2,1)}), bf16[8,2,16384]{2,1,0:T(2,128)(2,1)S(1)}, u32[]{:S(2)}, u32[]{:S(2)}) %all-to-all-start) | async-done | bytes 524320 | tf_op jit(solution)/shard_map/all_to_all | solution.py:29
  58.8 0.5 reshape.54
  59.3 3.2 %reduce = bf16[8,32768]{1,0:T(8,128)(2,1)S(1)} reduce(bf16[8,1,32768]{2,1,0:T(2,128)(2,1)S(1)} %reshape.54, bf16[]{:T(256)} %constant.39), dimensions={1}, to_apply=%all_to_all.13.reduce_sub_computation | reduce | bytes 1048578 | tf_op jit(solution)/shard_map/all_to_all | solution.py:29
  62.5 0.2 reshape.46
  62.7 0.0 all-gather.2.cloned.1.call-done
  62.8 4.4 %convolution_multiply_fusion = f32[512,2048]{1,0:T(8,128)} fusion(bf16[2048,256]{0,1:T(8,128)(2,1)} %all-gather.2.cloned.1.call-done, bf16[1024,256]{1,0:T(8,128)(2,1)S(1)} %reshape.46, bf16[512,1024]{1,0:T(8,128)(2,1)S(1)} %copy-done, f32[256]{0:T(256)S(1)} %compare_convert_fusion), kind=kOutput, calls=%fused_computation.4 | convolution fusion | flops 806617088 | bytes 6816768 | tf_op jit(solution)/shard_map/dot_general | solution.py:45
  (2 shorter events, 0.0 us)
Async XLA Ops:
  6.5 30.4 %copy-start = (bf16[512,1024]{1,0:T(8,128)(2,1)S(1)}, bf16[512,1024]{1,0:T(8,128)(2,1)}, u32[]{:S(2)}) copy-start(bf16[512,1024]{1,0:T(8,128)(2,1)} %param.8) | copy-start | bytes 3145732
  6.5 56.2 %all-gather.2.cloned.1.call-start = ((), (), s32[]{:S(2)}) async-start(), calls=%async_computation.2 | async-start | bytes 1310720 | tf_op jit(solution)/shard_map/all_gather | solution.py:47
  11.0 27.2 %copy-start.1 = (bf16[4,128,256]{2,1,0:T(8,128)(2,1)S(1)}, bf16[4,128,256]{2,1,0:T(8,128)(2,1)}, u32[]{:S(2)}) copy-start(bf16[4,128,256]{2,1,0:T(8,128)(2,1)} %param.6) | copy-start | bytes 786436
  11.4 27.0 %copy-start.2 = (s32[8,1]{0,1:T(1,128)S(1)}, s32[8,1]{0,1:T(1,128)}, u32[]{:S(2)}) copy-start(s32[8,1]{0,1:T(1,128)} %param.9) | copy-start | bytes 100
  36.7 7.9 %copy-start.3 = (s32[16]{0:T(128)S(1)}, s32[16]{0:T(128)}, u32[]{:S(2)}) copy-start(s32[16]{0:T(128)} %param.11) | copy-start | bytes 196
  41.0 17.8 %all-to-all-start = ((bf16[8,2,16384]{2,1,0:T(2,128)(2,1)}), bf16[8,2,16384]{2,1,0:T(2,128)(2,1)S(1)}, u32[]{:S(2)}, u32[]{:S(2)}) async-start(bf16[8,2,16384]{2,1,0:T(2,128)(2,1)} %reshape.53), calls=%async_computation | async-start | bytes 1048576 | tf_op jit(solution)/shard_map/all_to_all | solution.py:29
Sparse Core Ops, SparseCore 0:
  38.3 15.7 all-gather.1
where the time goes:
time: 74.4 us; the launch traced here: 74 us
  blocking collectives  21.6 us (29%)
  waiting for transfers between devices  14.1 us (19%)
  between operations  13.5 us (18%)
  other arithmetic  9.22 us (12%)
  matrix products  7 us (9%)
  local copies, waits for them, and re-layouts  4.99 us (7%)
  starting transfers between devices  3.59 us (5%)
    all_to_all x1, blocking collectives, body(): lax.all_to_all(send_virt, 'aux', split_axis=0, concat_axis=0, tiled=True)  21.6 us
    all_to_all x1, waiting for transfers between devices, body(): lax.all_to_all(send_occ, 'aux', split_axis=0, concat_axis=0, tiled=True)  14.1 us
    dot_general x1, matrix products, body(): lax.dot_general(half_occ, lax.all_gather(half_virt, 'grp', axis=0, tiled=...  4.43 us
    all_to_all x2, other arithmetic, body(): lax.all_to_all(send_occ, 'aux', split_axis=0, concat_axis=0, tiled=True)  4.19 us
    all_to_all x2, other arithmetic, body(): lax.all_to_all(send_virt, 'aux', split_axis=0, concat_axis=0, tiled=True)  4.19 us
    unnamed x14, local copies, waits for them, and re-layouts  3.99 us
    all_to_all x1, starting transfers between devices, body(): lax.all_to_all(send_occ, 'aux', split_axis=0, concat_axis=0, tiled=True)  3.59 us
  transfers between devices with their start and end apart: 2, of which 1 were waited for; matrix products, arithmetic and copies ran while one was open for 9% of the time, Pallas kernels for 0%

commit v1 on v0

v1 whole, which is shorter than its diff:
```python
import functools
import math

import jax
import jax.numpy as jnp
from jax import lax
from jax.experimental import pallas as pl
from jax.experimental.pallas import tpu as pltpu
from jax.sharding import PartitionSpec as P

group_width = 16
MESH = pl.DeviceIdType.MESH
chunks = 4
depth = 1024


def route(
    n, idx_ref, live_ref, counts_ref, occ_ref, virt_ref, tc_hbm,
    half_occ, half_virt,
    send, stack, tc, load_sem, send_sem, recv_sem, pass_sem, got_sem, gs_sem, gr_sem,
):
    me = lax.axis_index("aux")
    g = lax.axis_index("grp")
    row, core = g // 2, g % 2
    twin = row * 2 + (1 - core)
    across = (1 - row) * 2 + core
    opposite = (1 - row) * 2 + (1 - core)
    size = virt_ref.shape[1]
    part = size // 2
    rows = tc.shape[0]
    step = rows // chunks

    load = pltpu.make_async_copy(tc_hbm, tc, load_sem.at[0])
    load.start()

    barrier = pltpu.get_barrier_semaphore()

    @pl.loop(1, n)
    def _(k):
        pl.semaphore_signal(
            barrier, inc=1, device_id={"aux": lax.rem(me + k, n)}, device_id_type=MESH
        )

    for peer in (twin, across):
        pl.semaphore_signal(barrier, inc=1, device_id={"grp": peer}, device_id_type=MESH)

    mine = pl.multiple_of(core * part, part)

    def stage(a):
        blocks = (virt_ref, occ_ref)[a]

        @pl.loop(1, n)
        def _(k):
            t = lax.rem(me + k, n)
            keep = live_ref[t, 0].astype(jnp.float32)
            piece = blocks[idx_ref[t, 0], pl.ds(mine, part), :]
            send[a, t] = (piece.astype(jnp.float32) * keep).astype(jnp.bfloat16)

        keep = live_ref[me, 0].astype(jnp.float32)
        own = blocks[idx_ref[me, 0]]
        stack[a, pl.ds(pl.multiple_of(me * size, size), size), :] = (
            own.astype(jnp.float32) * keep
        ).astype(jnp.bfloat16)

    def out_copy(a, t):
        here = pl.ds(pl.multiple_of(me * size + core * part, part), part)
        return pltpu.make_async_remote_copy(
            send.at[a, t], stack.at[a, here, :], send_sem.at[a, t], recv_sem.at[a, me],
            device_id={"aux": t}, device_id_type=MESH,
        )

    def in_copy(a, s):
        there = pl.ds(pl.multiple_of(s * size + core * part, part), part)
        return pltpu.make_async_remote_copy(
            send.at[a, s], stack.at[a, there, :], send_sem.at[a, s], recv_sem.at[a, s],
            device_id={"aux": s}, device_id_type=MESH,
        )

    def pass_copy(a, s, side):
        spot = pl.ds(pl.multiple_of(s * size + side * part, part), part)
        return pltpu.make_async_remote_copy(
            stack.at[a, spot, :], stack.at[a, spot, :], pass_sem.at[a, s], got_sem.at[a, s],
            device_id={"grp": twin}, device_id_type=MESH,
        )

    def start_all(a):
        @pl.loop(1, n)
        def _(k):
            out_copy(a, lax.rem(me + k, n)).start()

    def sent_all(a):
        @pl.loop(1, n)
        def _(k):
            out_copy(a, lax.rem(me + k, n)).wait_send()

    def pass_all(a):
        @pl.loop(1, n)
        def _(k):
            s = lax.rem(me + n - k, n)
            in_copy(a, s).wait_recv()
            pass_copy(a, s, core).start()

    def got_all(a):
        @pl.loop(1, n)
        def _(k):
            s = lax.rem(me + n - k, n)
            pass_copy(a, s, 1 - core).wait_recv()
            pass_copy(a, s, core).wait_send()

    def product(a, first):
        wide = tc.shape[1]
        deep = min(depth, wide)

        def term(i, total):
            at = pl.ds(pl.multiple_of(i * deep, deep), deep)
            return total + jnp.dot(
                tc[first : first + step, at], stack[a, at, :], preferred_element_type=jnp.float32
            )

        if wide == deep:
            return jnp.dot(
                tc[first : first + step, :], stack[a], preferred_element_type=jnp.float32
            )
        return lax.fori_loop(
            0, wide // deep, term, jnp.zeros((step, stack.shape[2]), jnp.float32)
        )

    def gather_copy(kind, origin, j, peer):
        spot = pl.ds(pl.multiple_of(origin * rows + j * step, step), step)
        return pltpu.make_async_remote_copy(
            half_virt.at[spot, :], half_virt.at[spot, :], gs_sem.at[kind, j], gr_sem.at[kind, j],
            device_id={"grp": peer}, device_id_type=MESH,
        )

    stage(0)
    pl.semaphore_wait(barrier, n + 1)
    start_all(0)
    stage(1)
    sent_all(0)
    start_all(1)
    pass_all(0)
    load.wait()
    got_all(0)
    for j in range(chunks):
        spot = pl.ds(pl.multiple_of(g * rows + j * step, step), step)
        half_virt[spot, :] = product(0, j * step).astype(jnp.bfloat16)
        gather_copy(0, g, j, across).start()
        gather_copy(1, g, j, twin).start()
    pass_all(1)
    for j in range(chunks):
        gather_copy(0, across, j, across).wait_recv()
        gather_copy(2, across, j, twin).start()
    got_all(1)

    column = lax.broadcasted_iota(jnp.int32, (1, stack.shape[2]), 1)
    owner = column // group_width
    limit = jnp.zeros_like(column)
    for q in range(counts_ref.shape[0]):
        limit = jnp.where(owner == q, counts_ref[q], limit)
    mask = jnp.where(column - owner * group_width < limit, 1.0, 0.0).astype(jnp.float32)
    for j in range(chunks):
        half_occ[j * step : (j + 1) * step, :] = (product(1, j * step) * mask).astype(jnp.bfloat16)

    sent_all(1)
    for j in range(chunks):
        gather_copy(0, g, j, across).wait_send()
        gather_copy(1, g, j, twin).wait_send()
        gather_copy(1, twin, j, twin).wait_recv()
        gather_copy(2, across, j, twin).wait_send()
        gather_copy(2, opposite, j, twin).wait_recv()


def body(occ_blocks, virt_blocks, three_center, blk_index, blk_live, live_counts):
    n = lax.axis_size("aux")
    parts = lax.axis_size("grp")
    _, size, width = occ_blocks.shape
    rows, slots = three_center.shape
    scale = 1.0 / math.sqrt(width)
    smem = pl.BlockSpec(memory_space=pltpu.SMEM)
    hbm = pl.BlockSpec(memory_space=pl.ANY)
    vmem = pl.BlockSpec(memory_space=pltpu.VMEM)
    dma = pltpu.SemaphoreType.DMA
    half_occ, half_virt = pl.pallas_call(
        functools.partial(route, n),
        out_shape=(
            jax.ShapeDtypeStruct((rows, width), jnp.bfloat16),
            jax.ShapeDtypeStruct((parts * rows, width), jnp.bfloat16),
        ),
        in_specs=[smem, smem, smem, vmem, vmem, hbm],
        out_specs=(vmem, vmem),
        scratch_shapes=[
            pltpu.VMEM((2, n, size // 2, width), jnp.bfloat16),
            pltpu.VMEM((2, n * size, width), jnp.bfloat16),
            pltpu.VMEM((rows, slots), jnp.bfloat16),
            dma((1,)),
            dma((2, n)), dma((2, n)), dma((2, n)), dma((2, n)),
            dma((3, chunks)), dma((3, chunks)),
        ],
        compiler_params=pltpu.CompilerParams(
            collective_id=0, has_side_effects=True, vmem_limit_bytes=48 * 1024 * 1024
        ),
        cost_estimate=pl.CostEstimate(
            flops=4 * rows * slots * width, bytes_accessed=2 * rows * slots, transcendentals=0
        ),
    )(blk_index, blk_live, live_counts, occ_blocks, virt_blocks, three_center)
    return (
        lax.dot_general(
            half_occ, half_virt, (((1,), (1,)), ((), ())), preferred_element_type=jnp.float32
        )
        * scale
    )


def solution(mesh):
    placed = (
        P("aux", None, None),
        P("aux", None, None),
        P(("aux", "grp"), None),
        P(None, "aux"),
        P(None, "aux"),
        P(),
    )
    return jax.shard_map(
        body, mesh=mesh, in_specs=placed, out_specs=P(("aux", "grp"), None), check_vma=False
    )
```

time: 74.4 us -> 34 us (0.46)
  the two profiles are of different devices: /device:TPU:0 before, /device:TPU:11 now
where the time goes in v1:
time: 34 us; the launch traced here: 33.7 us
  Pallas kernels  25.7 us (76%)
  local copies, waits for them, and re-layouts  5.24 us (15%)
  matrix products  2.76 us (8%)
    pallas_call x1, Pallas kernels, body(): pl.pallas_call(functools.partial(route, n), out_shape=(jax.ShapeDtypeStru...  25.7 us
    unnamed x10, local copies, waits for them, and re-layouts  5.24 us
    dot_general x1, matrix products, body(): lax.dot_general(half_occ, half_virt, (((1,), (1,)), ((), ())), preferred_...  2.76 us

profile of v1, /device:TPU:11, one launch (start us, length us, event | category | flops | bytes accessed | tf_op | source)
XLA Modules:
  0.0 33.7 jit_solution(10086002788420760946)
XLA Ops:
  0.0 0.7 %copy.7.idx_ref = s32[8,1]{1,0:T(8,128)S(1)} copy(s32[8,1]{0,1:T(1,128)} %param.9) | data formatting | bytes 64 | tf_op args[3]
  0.7 0.7 %copy.8.live_ref = s32[8,1]{1,0:T(8,128)S(1)} copy(s32[8,1]{0,1:T(1,128)} %param.10) | data formatting | bytes 64 | tf_op args[4]
  1.5 0.0 copy-start
  1.5 1.2 %copy-done = bf16[512,1024]{1,0:T(8,128)(2,1)S(1)} copy-done((bf16[512,1024]{1,0:T(8,128)(2,1)S(1)}, bf16[512,1024]{1,0:T(8,128)(2,1)}, u32[]{:S(2)}) %copy-start) | copy-done | bytes 1048600
  2.7 0.0 copy-start.1
  2.7 0.9 %copy-done.1 = bf16[4,128,256]{2,1,0:T(8,128)(2,1)S(1)} copy-done((bf16[4,128,256]{2,1,0:T(8,128)(2,1)S(1)}, bf16[4,128,256]{2,1,0:T(8,128)(2,1)}, u32[]{:S(2)}) %copy-start.1) | copy-done | bytes 262168
  3.6 0.0 copy-start.2
  3.6 0.9 %copy-done.2 = bf16[4,128,256]{2,1,0:T(8,128)(2,1)S(1)} copy-done((bf16[4,128,256]{2,1,0:T(8,128)(2,1)S(1)}, bf16[4,128,256]{2,1,0:T(8,128)(2,1)}, u32[]{:S(2)}) %copy-start.2) | copy-done | bytes 262168
  4.6 0.0 copy-start.3
  4.6 0.7 %copy-done.3 = s32[16]{0:T(128)S(1)} copy-done((s32[16]{0:T(128)S(1)}, s32[16]{0:T(128)}, u32[]{:S(2)}) %copy-start.3) | copy-done | bytes 88
  5.2 25.7 %shard_map.64 = (bf16[512,256]{1,0:T(8,128)(2,1)S(1)}, bf16[2048,256]{1,0:T(8,128)(2,1)S(1)}) custom-call(s32[8,1]{1,0:T(8,128)S(1)} %copy.7.idx_ref, s32[8,1]{1,0:T(8,128)S(1)} %copy.8.live_ref, s32[16]{0:T(128)S(1)} %copy-done.3, bf16[4,128,256]{2,1,0:T(8,128)(2,1)S(1)} %copy-done.1, bf16[4,128,256]{2,1,0:T(8,128)(2,1)S(1)} %copy-done.2, ...), custom_call_target="tpu_custom_call" | custom-call | flops 536870912 | bytes 1048576 | tf_op jit(solution)/shard_map/pallas_call | solution.py:183
  31.0 2.8 %convolution_multiply_fusion = f32[512,2048]{1,0:T(8,128)} fusion(bf16[512,256]{1,0:T(8,128)(2,1)S(1)} %get-tuple-element.7, bf16[2048,256]{1,0:T(8,128)(2,1)S(1)} %get-tuple-element.8), kind=kOutput, calls=%fused_computation | convolution fusion | flops 537919488 | bytes 5505024 | tf_op jit(solution)/shard_map/dot_general | solution.py:207
Async XLA Ops:
  1.5 1.2 %copy-start = (bf16[512,1024]{1,0:T(8,128)(2,1)S(1)}, bf16[512,1024]{1,0:T(8,128)(2,1)}, u32[]{:S(2)}) copy-start(bf16[512,1024]{1,0:T(8,128)(2,1)} %tc_hbm.1) | copy-start | bytes 3145732
  2.7 0.9 %copy-start.1 = (bf16[4,128,256]{2,1,0:T(8,128)(2,1)S(1)}, bf16[4,128,256]{2,1,0:T(8,128)(2,1)}, u32[]{:S(2)}) copy-start(bf16[4,128,256]{2,1,0:T(8,128)(2,1)} %occ_ref.1) | copy-start | bytes 786436
  3.6 0.9 %copy-start.2 = (bf16[4,128,256]{2,1,0:T(8,128)(2,1)S(1)}, bf16[4,128,256]{2,1,0:T(8,128)(2,1)}, u32[]{:S(2)}) copy-start(bf16[4,128,256]{2,1,0:T(8,128)(2,1)} %virt_ref.1) | copy-start | bytes 786436
  4.6 0.7 %copy-start.3 = (s32[16]{0:T(128)S(1)}, s32[16]{0:T(128)}, u32[]{:S(2)}) copy-start(s32[16]{0:T(128)} %counts_ref.1) | copy-start | bytes 196

commit v2 on v1

--- a/solution.py
+++ b/solution.py
@@ -15,9 +15,9 @@
 
 
 def route(
-    n, idx_ref, live_ref, counts_ref, occ_ref, virt_ref, tc_hbm,
+    n, idx_hbm, live_hbm, counts_hbm, occ_hbm, virt_hbm, tc_hbm,
     half_occ, half_virt,
-    send, stack, tc, load_sem, send_sem, recv_sem, pass_sem, got_sem, gs_sem, gr_sem,
+    idx_ref, live_ref, counts_ref, occ_ref, virt_ref, send, stack, tc, load_sem, send_sem, recv_sem, pass_sem, got_sem, gs_sem, gr_sem,
 ):
     me = lax.axis_index("aux")
     g = lax.axis_index("grp")
@@ -30,8 +30,15 @@
     rows = tc.shape[0]
     step = rows // chunks
 
-    load = pltpu.make_async_copy(tc_hbm, tc, load_sem.at[0])
-    load.start()
+    pairs = (
+        (idx_hbm, idx_ref), (live_hbm, live_ref), (counts_hbm, counts_ref),
+        (virt_hbm, virt_ref), (occ_hbm, occ_ref), (tc_hbm, tc),
+    )
+    loads = [
+        pltpu.make_async_copy(src, dst, load_sem.at[i]) for i, (src, dst) in enumerate(pairs)
+    ]
+    for load in loads:
+        load.start()
 
     barrier = pltpu.get_barrier_semaphore()
 
@@ -52,12 +59,12 @@
         @pl.loop(1, n)
         def _(k):
             t = lax.rem(me + k, n)
-            keep = live_ref[t, 0].astype(jnp.float32)
-            piece = blocks[idx_ref[t, 0], pl.ds(mine, part), :]
+            keep = live_ref[0, t].astype(jnp.float32)
+            piece = blocks[idx_ref[0, t], pl.ds(mine, part), :]
             send[a, t] = (piece.astype(jnp.float32) * keep).astype(jnp.bfloat16)
 
-        keep = live_ref[me, 0].astype(jnp.float32)
-        own = blocks[idx_ref[me, 0]]
+        keep = live_ref[0, me].astype(jnp.float32)
+        own = blocks[idx_ref[0, me]]
         stack[a, pl.ds(pl.multiple_of(me * size, size), size), :] = (
             own.astype(jnp.float32) * keep
         ).astype(jnp.bfloat16)
@@ -132,14 +139,17 @@
             device_id={"grp": peer}, device_id_type=MESH,
         )
 
+    for load in loads[:4]:
+        load.wait()
     stage(0)
     pl.semaphore_wait(barrier, n + 1)
     start_all(0)
+    loads[4].wait()
     stage(1)
     sent_all(0)
     start_all(1)
     pass_all(0)
-    load.wait()
+    loads[5].wait()
     got_all(0)
     for j in range(chunks):
         spot = pl.ds(pl.multiple_of(g * rows + j * step, step), step)
@@ -173,11 +183,10 @@
 def body(occ_blocks, virt_blocks, three_center, blk_index, blk_live, live_counts):
     n = lax.axis_size("aux")
     parts = lax.axis_size("grp")
-    _, size, width = occ_blocks.shape
+    local, size, width = occ_blocks.shape
     rows, slots = three_center.shape
     scale = 1.0 / math.sqrt(width)
-    smem = pl.BlockSpec(memory_space=pltpu.SMEM)
-    hbm = pl.BlockSpec(memory_space=pl.ANY)
+    hbm = pl.BlockSpec(memory_space=pltpu.HBM)
     vmem = pl.BlockSpec(memory_space=pltpu.VMEM)
     dma = pltpu.SemaphoreType.DMA
     half_occ, half_virt = pl.pallas_call(
@@ -186,13 +195,18 @@
             jax.ShapeDtypeStruct((rows, width), jnp.bfloat16),
             jax.ShapeDtypeStruct((parts * rows, width), jnp.bfloat16),
         ),
-        in_specs=[smem, smem, smem, vmem, vmem, hbm],
+        in_specs=[hbm] * 6,
         out_specs=(vmem, vmem),
         scratch_shapes=[
+            pltpu.SMEM((1, n), jnp.int32),
+            pltpu.SMEM((1, n), jnp.int32),
+            pltpu.SMEM(live_counts.shape, jnp.int32),
+            pltpu.VMEM((local, size, width), jnp.bfloat16),
+            pltpu.VMEM((local, size, width), jnp.bfloat16),
             pltpu.VMEM((2, n, size // 2, width), jnp.bfloat16),
             pltpu.VMEM((2, n * size, width), jnp.bfloat16),
             pltpu.VMEM((rows, slots), jnp.bfloat16),
-            dma((1,)),
+            dma((6,)),
             dma((2, n)), dma((2, n)), dma((2, n)), dma((2, n)),
             dma((3, chunks)), dma((3, chunks)),
         ],
@@ -202,7 +216,10 @@
         cost_estimate=pl.CostEstimate(
             flops=4 * rows * slots * width, bytes_accessed=2 * rows * slots, transcendentals=0
         ),
-    )(blk_index, blk_live, live_counts, occ_blocks, virt_blocks, three_center)
+    )(*[
+        pltpu.with_memory_space_constraint(x, pltpu.HBM)
+        for x in (blk_index.T, blk_live.T, live_counts, occ_blocks, virt_blocks, three_center)
+    ])
     return (
         lax.dot_general(
             half_occ, half_virt, (((1,), (1,)), ((), ())), preferred_element_type=jnp.float32

time: 34 us -> 27.9 us (0.82)
  local copies, waits for them, and re-layouts: 5.24 us -> 0 us
  Pallas kernels: 25.7 us -> 25 us
    unnamed x10 -> x0, local copies, waits for them, and re-layouts: 5.24 us -> none
    pallas_call x1, Pallas kernels: 25.7 us -> 25 us  [body(): pl.pallas_call(functools.partial(route, n), out_shape=(jax.ShapeDtypeStru...]
where the time goes in v2:
time: 27.9 us; the launch traced here: 27.7 us
  Pallas kernels  25 us (90%)
  matrix products  2.76 us (10%)
    pallas_call x1, Pallas kernels, body(): pl.pallas_call(functools.partial(route, n), out_shape=(jax.ShapeDtypeStru...  25 us
    dot_general x1, matrix products, body(): lax.dot_general(half_occ, half_virt, (((1,), (1,)), ((), ())), preferred_...  2.76 us

profile of v2, /device:TPU:11, one launch (start us, length us, event | category | flops | bytes accessed | tf_op | source)
XLA Modules:
  0.0 27.7 jit_solution(9985795737335321091)
XLA Ops:
  0.0 25.0 %shard_map.64 = (bf16[512,256]{1,0:T(8,128)(2,1)S(1)}, bf16[2048,256]{1,0:T(8,128)(2,1)S(1)}) custom-call(s32[1,8]{1,0:T(1,128)} %bitcast.4, s32[1,8]{1,0:T(1,128)} %bitcast.5, s32[16]{0:T(128)} %counts_hbm.1, bf16[4,128,256]{2,1,0:T(8,128)(2,1)} %occ_hbm.1, bf16[4,128,256]{2,1,0:T(8,128)(2,1)} %virt_hbm.1, bf16[512,1024]{1,0:T(8,128)(2,1)} %tc_hbm.1), custom_call_target="tpu_custom_call" | custom-call | flops 536870912 | bytes 1048576 | tf_op jit(solution)/shard_map/pallas_call | solution.py:192
  25.0 2.8 %convolution_multiply_fusion = f32[512,2048]{1,0:T(8,128)} fusion(bf16[512,256]{1,0:T(8,128)(2,1)S(1)} %get-tuple-element.7, bf16[2048,256]{1,0:T(8,128)(2,1)S(1)} %get-tuple-element.8), kind=kOutput, calls=%fused_computation | convolution fusion | flops 537919488 | bytes 5505024 | tf_op jit(solution)/shard_map/dot_general | solution.py:224

commit v3 on v2

--- a/solution.py
+++ b/solution.py
@@ -10,15 +10,17 @@
 
 group_width = 16
 MESH = pl.DeviceIdType.MESH
-chunks = 4
+chunks = 2
 depth = 1024
 
 
 def route(
     n, idx_hbm, live_hbm, counts_hbm, occ_hbm, virt_hbm, tc_hbm,
     half_occ, half_virt,
-    idx_ref, live_ref, counts_ref, occ_ref, virt_ref, send, stack, tc, load_sem, send_sem, recv_sem, pass_sem, got_sem, gs_sem, gr_sem,
+    idx_ref, live_ref, counts_ref, occ_ref, virt_ref, send_a, send_b, send_c, stack_a, stack_b, stack_c, tc, load_sem, send_sem, recv_sem, pass_sem, got_sem, gs_sem, gr_sem,
 ):
+    sends, stacks = (send_a, send_b, send_c), (stack_a, stack_b, stack_c)
+    half = stack_a.shape[1]
     me = lax.axis_index("aux")
     g = lax.axis_index("grp")
     row, core = g // 2, g % 2
@@ -54,39 +56,41 @@
     mine = pl.multiple_of(core * part, part)
 
     def stage(a):
-        blocks = (virt_ref, occ_ref)[a]
+        blocks = (virt_ref, virt_ref, occ_ref)[a]
+        cols = (slice(0, half), slice(half, 2 * half), slice(None))[a]
+        send, stack = sends[a], stacks[a]
 
         @pl.loop(1, n)
         def _(k):
             t = lax.rem(me + k, n)
             keep = live_ref[0, t].astype(jnp.float32)
-            piece = blocks[idx_ref[0, t], pl.ds(mine, part), :]
-            send[a, t] = (piece.astype(jnp.float32) * keep).astype(jnp.bfloat16)
+            piece = blocks[idx_ref[0, t], pl.ds(mine, part), cols]
+            send[t] = (piece.astype(jnp.float32) * keep).astype(jnp.bfloat16)
 
         keep = live_ref[0, me].astype(jnp.float32)
-        own = blocks[idx_ref[0, me]]
-        stack[a, pl.ds(pl.multiple_of(me * size, size), size), :] = (
+        own = blocks[idx_ref[0, me], :, cols]
+        stack[pl.ds(pl.multiple_of(me * size, size), size), :] = (
             own.astype(jnp.float32) * keep
         ).astype(jnp.bfloat16)
 
     def out_copy(a, t):
         here = pl.ds(pl.multiple_of(me * size + core * part, part), part)
         return pltpu.make_async_remote_copy(
-            send.at[a, t], stack.at[a, here, :], send_sem.at[a, t], recv_sem.at[a, me],
+            sends[a].at[t], stacks[a].at[here, :], send_sem.at[a, t], recv_sem.at[a, me],
             device_id={"aux": t}, device_id_type=MESH,
         )
 
     def in_copy(a, s):
         there = pl.ds(pl.multiple_of(s * size + core * part, part), part)
         return pltpu.make_async_remote_copy(
-            send.at[a, s], stack.at[a, there, :], send_sem.at[a, s], recv_sem.at[a, s],
+            sends[a].at[s], stacks[a].at[there, :], send_sem.at[a, s], recv_sem.at[a, s],
             device_id={"aux": s}, device_id_type=MESH,
         )
 
     def pass_copy(a, s, side):
         spot = pl.ds(pl.multiple_of(s * size + side * part, part), part)
         return pltpu.make_async_remote_copy(
-            stack.at[a, spot, :], stack.at[a, spot, :], pass_sem.at[a, s], got_sem.at[a, s],
+            stacks[a].at[spot, :], stacks[a].at[spot, :], pass_sem.at[a, s], got_sem.at[a, s],
             device_id={"grp": twin}, device_id_type=MESH,
         )
 
@@ -115,69 +119,86 @@
             pass_copy(a, s, core).wait_send()
 
     def product(a, first):
+        stack = stacks[a]
         wide = tc.shape[1]
         deep = min(depth, wide)
 
         def term(i, total):
             at = pl.ds(pl.multiple_of(i * deep, deep), deep)
             return total + jnp.dot(
-                tc[first : first + step, at], stack[a, at, :], preferred_element_type=jnp.float32
+                tc[first : first + step, at], stack[at, :], preferred_element_type=jnp.float32
             )
 
         if wide == deep:
             return jnp.dot(
-                tc[first : first + step, :], stack[a], preferred_element_type=jnp.float32
+                tc[first : first + step, :], stack[...], preferred_element_type=jnp.float32
             )
         return lax.fori_loop(
-            0, wide // deep, term, jnp.zeros((step, stack.shape[2]), jnp.float32)
-        )
-
-    def gather_copy(kind, origin, j, peer):
+            0, wide // deep, term, jnp.zeros((step, stack.shape[1]), jnp.float32)
+        )
+
+    def gather_copy(kind, origin, h, j, peer):
+        cols = slice(h * half, (h + 1) * half)
+        lane = h * chunks + j
         spot = pl.ds(pl.multiple_of(origin * rows + j * step, step), step)
         return pltpu.make_async_remote_copy(
-            half_virt.at[spot, :], half_virt.at[spot, :], gs_sem.at[kind, j], gr_sem.at[kind, j],
+            half_virt.at[spot, cols], half_virt.at[spot, cols], gs_sem.at[kind, lane], gr_sem.at[kind, lane],
             device_id={"grp": peer}, device_id_type=MESH,
         )
 
     for load in loads[:4]:
         load.wait()
+    def half_product(h):
+        for j in range(chunks):
+            spot = pl.ds(pl.multiple_of(g * rows + j * step, step), step)
+            half_virt[spot, h * half : (h + 1) * half] = product(h, j * step).astype(jnp.bfloat16)
+            gather_copy(0, g, h, j, across).start()
+            gather_copy(1, g, h, j, twin).start()
+
+    def relay(h):
+        for j in range(chunks):
+            gather_copy(0, across, h, j, across).wait_recv()
+            gather_copy(2, across, h, j, twin).start()
+
     stage(0)
     pl.semaphore_wait(barrier, n + 1)
     start_all(0)
+    stage(1)
     loads[4].wait()
-    stage(1)
+    stage(2)
     sent_all(0)
     start_all(1)
     pass_all(0)
     loads[5].wait()
     got_all(0)
-    for j in range(chunks):
-        spot = pl.ds(pl.multiple_of(g * rows + j * step, step), step)
-        half_virt[spot, :] = product(0, j * step).astype(jnp.bfloat16)
-        gather_copy(0, g, j, across).start()
-        gather_copy(1, g, j, twin).start()
+    half_product(0)
+    sent_all(1)
+    start_all(2)
     pass_all(1)
-    for j in range(chunks):
-        gather_copy(0, across, j, across).wait_recv()
-        gather_copy(2, across, j, twin).start()
     got_all(1)
-
-    column = lax.broadcasted_iota(jnp.int32, (1, stack.shape[2]), 1)
+    half_product(1)
+    relay(0)
+    relay(1)
+    pass_all(2)
+    got_all(2)
+
+    column = lax.broadcasted_iota(jnp.int32, (1, 2 * half), 1)
     owner = column // group_width
     limit = jnp.zeros_like(column)
     for q in range(counts_ref.shape[0]):
         limit = jnp.where(owner == q, counts_ref[q], limit)
     mask = jnp.where(column - owner * group_width < limit, 1.0, 0.0).astype(jnp.float32)
     for j in range(chunks):
-        half_occ[j * step : (j + 1) * step, :] = (product(1, j * step) * mask).astype(jnp.bfloat16)
-
-    sent_all(1)
-    for j in range(chunks):
-        gather_copy(0, g, j, across).wait_send()
-        gather_copy(1, g, j, twin).wait_send()
-        gather_copy(1, twin, j, twin).wait_recv()
-        gather_copy(2, across, j, twin).wait_send()
-        gather_copy(2, opposite, j, twin).wait_recv()
+        half_occ[j * step : (j + 1) * step, :] = (product(2, j * step) * mask).astype(jnp.bfloat16)
+
+    sent_all(2)
+    for h in range(2):
+        for j in range(chunks):
+            gather_copy(0, g, h, j, across).wait_send()
+            gather_copy(1, g, h, j, twin).wait_send()
+            gather_copy(1, twin, h, j, twin).wait_recv()
+            gather_copy(2, across, h, j, twin).wait_send()
+            gather_copy(2, opposite, h, j, twin).wait_recv()
 
 
 def body(occ_blocks, virt_blocks, three_center, blk_index, blk_live, live_counts):
@@ -185,6 +206,7 @@
     parts = lax.axis_size("grp")
     local, size, width = occ_blocks.shape
     rows, slots = three_center.shape
+    widths = (width // 2, width // 2, width)
     scale = 1.0 / math.sqrt(width)
     hbm = pl.BlockSpec(memory_space=pltpu.HBM)
     vmem = pl.BlockSpec(memory_space=pltpu.VMEM)
@@ -203,12 +225,12 @@
             pltpu.SMEM(live_counts.shape, jnp.int32),
             pltpu.VMEM((local, size, width), jnp.bfloat16),
             pltpu.VMEM((local, size, width), jnp.bfloat16),
-            pltpu.VMEM((2, n, size // 2, width), jnp.bfloat16),
-            pltpu.VMEM((2, n * size, width), jnp.bfloat16),
+            *[pltpu.VMEM((n, size // 2, w), jnp.bfloat16) for w in widths],
+            *[pltpu.VMEM((n * size, w), jnp.bfloat16) for w in widths],
             pltpu.VMEM((rows, slots), jnp.bfloat16),
             dma((6,)),
-            dma((2, n)), dma((2, n)), dma((2, n)), dma((2, n)),
-            dma((3, chunks)), dma((3, chunks)),
+            dma((3, n)), dma((3, n)), dma((3, n)), dma((3, n)),
+            dma((3, 2 * chunks)), dma((3, 2 * chunks)),
         ],
         compiler_params=pltpu.CompilerParams(
             collective_id=0, has_side_effects=True, vmem_limit_bytes=48 * 1024 * 1024

time: 27.9 us -> 25.1 us (0.90)
  the two profiles are of different devices: /device:TPU:11 before, /device:TPU:0 now
where the time goes in v3:
time: 25.1 us; the launch traced here: 24.9 us
  Pallas kernels  22.2 us (88%)
  matrix products  2.76 us (11%)
    pallas_call x1, Pallas kernels, body(): pl.pallas_call(functools.partial(route, n), out_shape=(jax.ShapeDtypeStru...  22.2 us
    dot_general x1, matrix products, body(): lax.dot_general(half_occ, half_virt, (((1,), (1,)), ((), ())), preferred_...  2.76 us

profile of v3, /device:TPU:0, one launch (start us, length us, event | category | flops | bytes accessed | tf_op | source)
XLA Modules:
  0.0 24.9 jit_solution(11953517577179448875)
XLA Ops:
  0.0 22.2 %shard_map.64 = (bf16[512,256]{1,0:T(8,128)(2,1)S(1)}, bf16[2048,256]{1,0:T(8,128)(2,1)S(1)}) custom-call(s32[1,8]{1,0:T(1,128)} %bitcast.4, s32[1,8]{1,0:T(1,128)} %bitcast.5, s32[16]{0:T(128)} %counts_hbm.1, bf16[4,128,256]{2,1,0:T(8,128)(2,1)} %occ_hbm.1, bf16[4,128,256]{2,1,0:T(8,128)(2,1)} %virt_hbm.1, bf16[512,1024]{1,0:T(8,128)(2,1)} %tc_hbm.1), custom_call_target="tpu_custom_call" | custom-call | flops 536870912 | bytes 1048576 | tf_op jit(solution)/shard_map/pallas_call | solution.py:214
  22.2 2.8 %convolution_multiply_fusion = f32[512,2048]{1,0:T(8,128)} fusion(bf16[512,256]{1,0:T(8,128)(2,1)S(1)} %get-tuple-element.7, bf16[2048,256]{1,0:T(8,128)(2,1)S(1)} %get-tuple-element.8), kind=kOutput, calls=%fused_computation | convolution fusion | flops 537919488 | bytes 5505024 | tf_op jit(solution)/shard_map/dot_general | solution.py:246

commit v4 on v3

--- a/solution.py
+++ b/solution.py
@@ -10,7 +10,7 @@
 
 group_width = 16
 MESH = pl.DeviceIdType.MESH
-chunks = 2
+chunks = 1
 depth = 1024
 
 

time: 25.1 us -> 25.5 us (1.016)
  Pallas kernels: 22.2 us -> 22.6 us
    pallas_call x1, Pallas kernels: 22.2 us -> 22.6 us  [body(): pl.pallas_call(functools.partial(route, n), out_shape=(jax.ShapeDtypeStru...]
where the time goes in v4:
time: 25.5 us; the launch traced here: 25.3 us
  Pallas kernels  22.6 us (89%)
  matrix products  2.76 us (11%)
    pallas_call x1, Pallas kernels, body(): pl.pallas_call(functools.partial(route, n), out_shape=(jax.ShapeDtypeStru...  22.6 us
    dot_general x1, matrix products, body(): lax.dot_general(half_occ, half_virt, (((1,), (1,)), ((), ())), preferred_...  2.76 us

profile of v4, /device:TPU:0, one launch (start us, length us, event | category | flops | bytes accessed | tf_op | source)
XLA Modules:
  0.0 25.3 jit_solution(8502749725883703887)
XLA Ops:
  0.0 22.6 %shard_map.64 = (bf16[512,256]{1,0:T(8,128)(2,1)S(1)}, bf16[2048,256]{1,0:T(8,128)(2,1)S(1)}) custom-call(s32[1,8]{1,0:T(1,128)} %bitcast.4, s32[1,8]{1,0:T(1,128)} %bitcast.5, s32[16]{0:T(128)} %counts_hbm.1, bf16[4,128,256]{2,1,0:T(8,128)(2,1)} %occ_hbm.1, bf16[4,128,256]{2,1,0:T(8,128)(2,1)} %virt_hbm.1, bf16[512,1024]{1,0:T(8,128)(2,1)} %tc_hbm.1), custom_call_target="tpu_custom_call" | custom-call | flops 536870912 | bytes 1048576 | tf_op jit(solution)/shard_map/pallas_call | solution.py:214
  22.6 2.8 %convolution_multiply_fusion = f32[512,2048]{1,0:T(8,128)} fusion(bf16[512,256]{1,0:T(8,128)(2,1)S(1)} %get-tuple-element.7, bf16[2048,256]{1,0:T(8,128)(2,1)S(1)} %get-tuple-element.8), kind=kOutput, calls=%fused_computation | convolution fusion | flops 537919488 | bytes 5505024 | tf_op jit(solution)/shard_map/dot_general | solution.py:246
